TPU v7x, 768 devices: a whole 4x8x12 slice. The times are simulated.
768 devices in a mesh: ctx: 12 (over z), head: 64 (over x, y, core).
Axes of the slice: x: 4, y: 8, z: 12, core: 2. Of those that a mesh axis runs over, the one named last changes fastest.
Arguments:
- queries: bfloat16 [8, 8, 12, 64, 12, 256], P(None, None, 'ctx', 'head'), may hold values from -6 to 6
- keys: bfloat16 [8, 8, 12, 64, 12, 256], P(None, None, 'ctx', 'head'), may hold values from -6 to 6
- values: bfloat16 [8, 8, 12, 64, 12, 256], P(None, None, 'ctx', 'head'), may hold values from -6 to 6
- gates: bfloat16 [8, 8, 12, 64, 12, 256], P(None, None, 'ctx', 'head'), may hold values from -6 to 6
- out_grad: bfloat16 [8, 8, 12, 64, 12, 256], P(None, None, 'ctx', 'head'), may hold values from -6 to 6
- gains: float32 [8, 256], replicated, may hold values from 0.5 to 1.5
Outputs:
- grad_queries: bfloat16 [8, 8, 12, 64, 12, 256], P(None, None, 'ctx', 'head')
- grad_keys: bfloat16 [8, 8, 12, 64, 12, 256], P(None, None, 'ctx', 'head')
- grad_values: bfloat16 [8, 8, 12, 64, 12, 256], P(None, None, 'ctx', 'head')
All inputs are finite; a program needn't handle non-finite values.
Results may differ from a plain program's by a relative error of at most 0.007.
Values may be sent and summed in bfloat16 or wider, within the bound.
No kernel may reach another device: no remote copies, remote signals or barrier semaphores. Data moves between devices by JAX's collectives and lax.ppermute only.
A program may use at most 64 MiB of HBM per device.

v0:
```python
import jax
import jax.numpy as jnp
from jax import lax
from jax.sharding import PartitionSpec as P


def entering(value, axis, join, neutral, backward):
    count, mine = (lax.axis_size(axis), lax.axis_index(axis))
    pieces = lax.all_gather(value, axis)
    if backward:
        pieces = pieces[::-1]
        mine = count - 1 - mine
    subtotal = jnp.full_like(value, 0) + jnp.asarray(neutral, value.dtype)

    def step(position, subtotal):
        longer = join(subtotal, pieces[position])
        return jnp.where(position < mine, longer, subtotal)

    return lax.fori_loop(0, count - 1, step, subtotal)


def shifted(block, axis, distance):
    devices = range(lax.axis_size(axis))
    route = [(i - distance, i) for i in devices if i - distance in devices]
    return lax.ppermute(block, axis, route)


def by_part(array):
    return array.reshape((array.shape[0] * array.shape[1], array.shape[4], array.shape[5]))


def add_states(earlier, later_one):
    return earlier + later_one


def carry_states(state, reverse, heads):
    empty = jnp.zeros_like(state)
    along = entering(state, "ctx", add_states, empty, reverse)
    total = lax.psum(state, "ctx")
    split_rows = lax.axis_size("head") // heads
    running = total
    stride = 1
    while stride < split_rows:
        offset = heads * stride
        if reverse:
            offset = -offset
        running = running + shifted(running, "head", offset)
        stride = stride * 2
    return along + (running - total)


def local(queries, keys, values, gates, out_grad, gains):
    f32 = jnp.float32
    bf16 = jnp.bfloat16
    shape = queries.shape
    heads = shape[1]
    device_row = lax.axis_index("head")
    head_id = device_row % heads
    q_all, k_all, v_all, g_all, d_all = (
        lax.all_to_all(by_part(queries), "head", split_axis=0, concat_axis=1, tiled=True),
        lax.all_to_all(by_part(keys), "head", split_axis=0, concat_axis=1, tiled=True),
        lax.all_to_all(by_part(values), "head", split_axis=0, concat_axis=1, tiled=True),
        lax.all_to_all(by_part(gates), "head", split_axis=0, concat_axis=1, tiled=True),
        lax.all_to_all(by_part(out_grad), "head", split_axis=0, concat_axis=1, tiled=True),
    )
    q = q_all[0]
    k = k_all[0]
    v = v_all[0]
    rows = q.shape[0]
    causal = jnp.arange(rows)[:, None] >= jnp.arange(rows)[None, :]
    state = jnp.einsum("se,sf->ef", k, v, preferred_element_type=f32)
    carried = carry_states(state, False, heads)
    gate_rows = g_all[0]
    dout = d_all[0]
    carried_low = carried.astype(bf16)
    scores = jnp.einsum("te,se->ts", q, k, preferred_element_type=f32)
    masked = jnp.where(causal, scores, 0.0).astype(bf16)
    mixed = jnp.dot(q, carried_low, preferred_element_type=f32) + jnp.dot(
        masked, v, preferred_element_type=f32
    )
    gain = lax.dynamic_slice_in_dim(gains, head_id, 1, 0)[0]
    inv = lax.rsqrt(jnp.mean(mixed * mixed, -1, keepdims=True) + 1e-05)
    normed = mixed * inv
    dnormed = dout.astype(f32) * gain[None, :] * jax.nn.silu(gate_rows.astype(f32))
    dmixed = (inv * (dnormed - normed * jnp.mean(dnormed * normed, -1, keepdims=True))).astype(bf16)
    back_state = jnp.einsum("te,tf->ef", q, dmixed, preferred_element_type=f32)
    later = carry_states(back_state, True, heads)
    later_low = later.astype(bf16)
    across = jnp.einsum("tf,sf->ts", dmixed, v, preferred_element_type=f32)
    across = jnp.where(causal, across, 0.0).astype(bf16)
    grad_q = jnp.einsum("tf,ef->te", dmixed, carried_low, preferred_element_type=f32) + jnp.dot(
        across, k, preferred_element_type=f32
    )
    grad_k = jnp.einsum("sf,ef->se", v, later_low, preferred_element_type=f32) + jnp.einsum(
        "ts,te->se", across, q, preferred_element_type=f32
    )
    grad_v = jnp.dot(k, later_low, preferred_element_type=f32) + jnp.einsum(
        "ts,tf->sf", masked, dmixed, preferred_element_type=f32
    )
    back_q, back_k, back_v = (
        lax.all_to_all(grad_q.astype(bf16)[None], "head", split_axis=1, concat_axis=0, tiled=True),
        lax.all_to_all(grad_k.astype(bf16)[None], "head", split_axis=1, concat_axis=0, tiled=True),
        lax.all_to_all(grad_v.astype(bf16)[None], "head", split_axis=1, concat_axis=0, tiled=True),
    )
    return (back_q.reshape(shape), back_k.reshape(shape), back_v.reshape(shape))


def solution(mesh):
    placed = (
        P(None, None, "ctx", "head", None, None),
        P(None, None, "ctx", "head", None, None),
        P(None, None, "ctx", "head", None, None),
        P(None, None, "ctx", "head", None, None),
        P(None, None, "ctx", "head", None, None),
        P(),
    )
    return jax.shard_map(
        local,
        mesh=mesh,
        in_specs=placed,
        out_specs=(
            P(None, None, "ctx", "head", None, None),
            P(None, None, "ctx", "head", None, None),
            P(None, None, "ctx", "head", None, None),
        ),
        check_vma=False,
    )
```

profile of v0, /device:TPU:1, one launch (start us, length us, event | category | flops | bytes accessed | tf_op | source)
XLA Modules:
  0.0 582.9 jit_solution(11474256571168257697)
XLA Ops:
  9.1 14.7 %all-to-all-start = ((bf16[64,12,256]{2,1,0:T(8,128)(2,1)}), bf16[64,12,256]{2,1,0:T(8,128)(2,1)S(1)}, u32[]{:S(2)}, u32[]{:S(2)}) async-start(bf16[64,12,256]{2,1,0:T(8,128)(2,1)} %bitcast), calls=%async_computation | async-start | bytes 1048576 | tf_op jit(solution)/shard_map/all_to_all | solution.py:61
  25.0 16.2 %all-to-all-done = bf16[64,12,256]{2,1,0:T(8,128)(2,1)S(1)} async-done(((bf16[64,12,256]{2,1,0:T(8,128)(2,1)}), bf16[64,12,256]{2,1,0:T(8,128)(2,1)S(1)}, u32[]{:S(2)}, u32[]{:S(2)}) %all-to-all-start) | async-done | bytes 393248 | tf_op jit(solution)/shard_map/all_to_all | solution.py:61
  41.2 23.5 %all_to_all.32 = bf16[64,12,256]{2,1,0:T(8,128)(2,1)S(1)} all-to-all(bf16[64,12,256]{2,1,0:T(8,128)(2,1)S(1)} %bitcast.75), channel_id=1, replica_groups=mesh['ctx'=12,'head'=64] {'head'}, dimensions={0} | all-to-all | bytes 786432 | tf_op jit(solution)/shard_map/all_to_all | solution.py:62
  67.7 6.3 %all-to-all-start.4 = ((bf16[64,12,256]{2,1,0:T(8,128)(2,1)}), bf16[64,12,256]{2,1,0:T(8,128)(2,1)S(1)}, u32[]{:S(2)}, u32[]{:S(2)}) async-start(bf16[64,12,256]{2,1,0:T(8,128)(2,1)} %copy.50), calls=%async_computation.4 | async-start | bytes 1048576 | tf_op jit(solution)/shard_map/all_to_all | solution.py:63
  75.0 16.2 %all-to-all-done.4 = bf16[64,12,256]{2,1,0:T(8,128)(2,1)S(1)} async-done(((bf16[64,12,256]{2,1,0:T(8,128)(2,1)}), bf16[64,12,256]{2,1,0:T(8,128)(2,1)S(1)}, u32[]{:S(2)}, u32[]{:S(2)}) %all-to-all-start.4) | async-done | bytes 393248 | tf_op jit(solution)/shard_map/all_to_all | solution.py:63
  91.3 6.3 %all-to-all-start.3 = ((bf16[64,12,256]{2,1,0:T(8,128)(2,1)}), bf16[64,12,256]{2,1,0:T(8,128)(2,1)S(1)}, u32[]{:S(2)}, u32[]{:S(2)}) async-start(bf16[64,12,256]{2,1,0:T(8,128)(2,1)} %copy.47), calls=%async_computation.3 | async-start | bytes 1048576 | tf_op jit(solution)/shard_map/all_to_all | solution.py:64
  98.6 16.3 %all-to-all-done.3 = bf16[64,12,256]{2,1,0:T(8,128)(2,1)S(1)} async-done(((bf16[64,12,256]{2,1,0:T(8,128)(2,1)}), bf16[64,12,256]{2,1,0:T(8,128)(2,1)S(1)}, u32[]{:S(2)}, u32[]{:S(2)}) %all-to-all-start.3) | async-done | bytes 393248 | tf_op jit(solution)/shard_map/all_to_all | solution.py:64
  114.9 6.5 %all-to-all-start.2 = ((bf16[64,12,256]{2,1,0:T(8,128)(2,1)}), bf16[64,12,256]{2,1,0:T(8,128)(2,1)}, u32[]{:S(2)}, u32[]{:S(2)}) async-start(bf16[64,12,256]{2,1,0:T(8,128)(2,1)} %copy.45), calls=%async_computation.2 | async-start | bytes 1048576 | tf_op jit(solution)/shard_map/all_to_all | solution.py:60
  121.4 2.4 all-gather.5.cloned.1.call-done
  124.6 111.4 %all-reduce.3.cloned.1.call-done = f32[256,256]{1,0:T(8,128)} async-done(((f32[256,256]{1,0:T(8,128)}), f32[256,256]{1,0:T(8,128)}) %all-reduce.3.cloned.1.call-update) | async-done | bytes 262160 | tf_op jit(solution)/shard_map/psum | solution.py:39
  235.9 7.8 %collective-permute-start = (f32[256,256]{1,0:T(8,128)}, f32[256,256]{1,0:T(8,128)}, u32[]{:S(2)}, u32[]{:S(2)}) collective-permute-start(f32[256,256]{1,0:T(8,128)} %all-reduce.3.cloned.1.call-done), channel_id=1, source_target_pairs={{0,8},{1,9},{2,10},{3,11},{4,12},{5,13},{6,14},{7,15},{8,16},{9,17... | collective-permute-start | bytes 786440 | tf_op jit(solution)/shard_map/ppermute | solution.py:25
  250.5 3.8 collective-permute-start.1
  255.8 3.1 collective-permute-done.1
  259.6 6.0 %collective-permute-start.2 = (f32[256,256]{1,0:T(8,128)}, f32[256,256]{1,0:T(8,128)}, u32[]{:S(2)}, u32[]{:S(2)}) collective-permute-start(f32[256,256]{1,0:T(8,128)} %add.119), channel_id=1, source_target_pairs={{0,32},{1,33},{2,34},{3,35},{4,36},{5,37},{6,38},{7,39},{8,40},{9,... | collective-permute-start | bytes 786440 | tf_op jit(solution)/shard_map/ppermute | solution.py:25
  265.7 11.7 %while.28 = (s32[]{:T(128)}, f32[256,256]{1,0:T(8,128)S(1)}, s32[]{:T(128)}, f32[12,256,256]{2,1,0:T(8,128)}, s32[]{:T(128)}, /*index=5*/s32[]{:T(128)}) while((s32[]{:T(128)}, f32[256,256]{1,0:T(8,128)S(1)}, s32[]{:T(128)}, f32[12,256,256]{2,1,0:T(8,128)}, s32[]{:T(128)}, /*index=5*/s32[]{:T(128)}) %tuple.81), condition=%wide.region_1.2_spmd.clone, body=%wide.region_0.1_spmd.clone.sunk | while | flops 196612 | bytes 786533 | solution.py:19
  281.3 62.7 %all-gather.7.cloned.1.call-done = f32[3072,256]{0,1:T(8,128)} async-done(((f32[256,256]{0,1:T(8,128)}), f32[3072,256]{0,1:T(8,128)}) %all-gather.7.cloned.1.call-update) | async-done | bytes 3145744 | tf_op jit(solution)/shard_map/all_gather | solution.py:9
  344.6 111.4 %all-reduce.5.cloned.1.call-done = f32[256,256]{0,1:T(8,128)} async-done(((f32[256,256]{0,1:T(8,128)}), f32[256,256]{0,1:T(8,128)}) %all-reduce.5.cloned.1.call-update) | async-done | bytes 262160 | tf_op jit(solution)/shard_map/psum | solution.py:39
  457.9 9.5 %collective-permute-done.3 = f32[256,256]{0,1:T(8,128)S(1)} collective-permute-done((f32[256,256]{0,1:T(8,128)}, f32[256,256]{0,1:T(8,128)S(1)}, u32[]{:S(2)}, u32[]{:S(2)}) %collective-permute-start.3) | collective-permute-done | bytes 262176 | tf_op jit(solution)/shard_map/ppermute | solution.py:25
  471.6 3.1 reduce.6
  475.6 24.5 %all-to-all-start.5 = ((bf16[64,2,1536]{2,1,0:T(2,128)(2,1)}), bf16[64,2,1536]{2,1,0:T(2,128)(2,1)}, u32[]{:S(2)}, u32[]{:S(2)}) async-start(bf16[64,2,1536]{2,1,0:T(2,128)(2,1)} %reshape.94), calls=%async_computation.5 | async-start | bytes 786432 | tf_op jit(solution)/shard_map/all_to_all | solution.py:101
  500.1 2.4 copy.54
  507.0 11.8 %while.29 = (s32[]{:T(128)}, f32[256,256]{1,0:T(8,128)S(1)}, s32[]{:T(128)}, f32[12,256,256]{2,1,0:T(8,128)}, s32[]{:T(128)}, /*index=5*/s32[]{:T(128)}) while((s32[]{:T(128)}, f32[256,256]{1,0:T(8,128)S(1)}, s32[]{:T(128)}, f32[12,256,256]{2,1,0:T(8,128)}, s32[]{:T(128)}, /*index=5*/s32[]{:T(128)}) %tuple.70), condition=%wide.region_6.7_spmd.clone, body=%wide.region_5.6_spmd.clone.sunk | while | flops 196612 | bytes 786533 | solution.py:19
  521.3 3.1 reduce.8
  525.3 12.0 %all-to-all-start.7 = ((bf16[64,2,1536]{2,1,0:T(2,128)(2,1)}), bf16[64,2,1536]{2,1,0:T(2,128)(2,1)S(1)}, u32[]{:S(2)}, u32[]{:S(2)}) async-start(bf16[64,2,1536]{2,1,0:T(2,128)(2,1)} %reshape.98), calls=%async_computation.7 | async-start | bytes 786432 | tf_op jit(solution)/shard_map/all_to_all | solution.py:103
  538.9 3.1 reduce.7
  542.9 9.1 %all-to-all-done.7 = bf16[64,2,1536]{2,1,0:T(2,128)(2,1)S(1)} async-done(((bf16[64,2,1536]{2,1,0:T(2,128)(2,1)}), bf16[64,2,1536]{2,1,0:T(2,128)(2,1)S(1)}, u32[]{:S(2)}, u32[]{:S(2)}) %all-to-all-start.7) | async-done | bytes 393248 | tf_op jit(solution)/shard_map/all_to_all | solution.py:103
  552.0 6.2 %all-to-all-start.6 = ((bf16[64,2,1536]{2,1,0:T(2,128)(2,1)}), bf16[64,2,1536]{2,1,0:T(2,128)(2,1)S(1)}, u32[]{:S(2)}, u32[]{:S(2)}) async-start(bf16[64,2,1536]{2,1,0:T(2,128)(2,1)} %reshape.96), calls=%async_computation.6 | async-start | bytes 786432 | tf_op jit(solution)/shard_map/all_to_all | solution.py:102
  558.2 2.7 reshape.95
  560.9 2.3 bitcast_reduce_fusion.2
  564.5 2.3 bitcast_reduce_fusion
  567.8 5.0 all-to-all-done.6
  573.1 2.3 bitcast_reduce_fusion.1
  (144 shorter events, 66.0 us)
Async XLA Ops:
  7.2 236.5 %copy-start = (f32[8,256]{1,0:T(8,128)S(1)}, f32[8,256]{1,0:T(8,128)}, u32[]{:S(2)}) copy-start(f32[8,256]{1,0:T(8,128)} %param.15) | copy-start | bytes 24580
  9.1 57.5 %copy-start.21 = (bf16[8,8,1,1,12,256]{5,1,4,3,2,0:T(8,128)(2,1)S(1)}, bf16[8,8,1,1,12,256]{5,1,4,3,2,0:T(8,128)(2,1)}, u32[]{:S(2)}) copy-start(bf16[8,8,1,1,12,256]{5,1,4,3,2,0:T(8,128)(2,1)} %param.13) | copy-start | bytes 1179652
  9.1 32.1 %all-to-all-start = ((bf16[64,12,256]{2,1,0:T(8,128)(2,1)}), bf16[64,12,256]{2,1,0:T(8,128)(2,1)S(1)}, u32[]{:S(2)}, u32[]{:S(2)}) async-start(bf16[64,12,256]{2,1,0:T(8,128)(2,1)} %bitcast), calls=%async_computation | async-start | bytes 1048576 | tf_op jit(solution)/shard_map/all_to_all | solution.py:61
  23.8 100.0 %all-gather.5.cloned.1.call-start = ((), (), s32[]{:S(2)}) async-start(), calls=%async_computation.10 | async-start | bytes 3407872 | tf_op jit(solution)/shard_map/all_gather | solution.py:9
  66.6 30.9 %copy-start.23 = (bf16[8,8,1,1,12,256]{5,1,4,3,2,0:T(8,128)(2,1)S(1)}, bf16[8,8,1,1,12,256]{5,1,4,3,2,0:T(8,128)(2,1)}, u32[]{:S(2)}) copy-start(bf16[8,8,1,1,12,256]{5,1,4,3,2,0:T(8,128)(2,1)} %param.10) | copy-start | bytes 1179652
  67.7 23.6 %all-to-all-start.4 = ((bf16[64,12,256]{2,1,0:T(8,128)(2,1)}), bf16[64,12,256]{2,1,0:T(8,128)(2,1)S(1)}, u32[]{:S(2)}, u32[]{:S(2)}) async-start(bf16[64,12,256]{2,1,0:T(8,128)(2,1)} %copy.50), calls=%async_computation.4 | async-start | bytes 1048576 | tf_op jit(solution)/shard_map/all_to_all | solution.py:63
  91.3 23.6 %all-to-all-start.3 = ((bf16[64,12,256]{2,1,0:T(8,128)(2,1)}), bf16[64,12,256]{2,1,0:T(8,128)(2,1)S(1)}, u32[]{:S(2)}, u32[]{:S(2)}) async-start(bf16[64,12,256]{2,1,0:T(8,128)(2,1)} %copy.47), calls=%async_computation.3 | async-start | bytes 1048576 | tf_op jit(solution)/shard_map/all_to_all | solution.py:64
  114.9 128.8 %copy-start.15 = (bf16[64,12,256]{2,1,0:T(8,128)(2,1)}, bf16[64,12,256]{2,1,0:T(8,128)(2,1)S(1)}, u32[]{:S(2)}) copy-start(bf16[64,12,256]{2,1,0:T(8,128)(2,1)S(1)} %all-to-all-done.3) | copy-start | bytes 1179652
  114.9 133.3 %all-to-all-start.2 = ((bf16[64,12,256]{2,1,0:T(8,128)(2,1)}), bf16[64,12,256]{2,1,0:T(8,128)(2,1)}, u32[]{:S(2)}, u32[]{:S(2)}) async-start(bf16[64,12,256]{2,1,0:T(8,128)(2,1)} %copy.45), calls=%async_computation.2 | async-start | bytes 1048576 | tf_op jit(solution)/shard_map/all_to_all | solution.py:60
  123.8 112.1 %all-reduce.3.cloned.1.call-start = ((), (), s32[]{:S(2)}) async-start(), calls=%async_computation.8 | async-start | bytes 524288 | tf_op jit(solution)/shard_map/psum | solution.py:39
  124.5 219.5 %all-gather.7.cloned.1.call-start = ((), (), s32[]{:S(2)}) async-start(), calls=%async_computation.11 | async-start | bytes 3407872 | tf_op jit(solution)/shard_map/all_gather | solution.py:9
  235.9 13.4 %collective-permute-start = (f32[256,256]{1,0:T(8,128)}, f32[256,256]{1,0:T(8,128)}, u32[]{:S(2)}, u32[]{:S(2)}) collective-permute-start(f32[256,256]{1,0:T(8,128)} %all-reduce.3.cloned.1.call-done), channel_id=1, source_target_pairs={{0,8},{1,9},{2,10},{3,11},{4,12},{5,13},{6,14},{7,15},{8,16},{9,17... | collective-permute-start | bytes 786440 | tf_op jit(solution)/shard_map/ppermute | solution.py:25
  249.3 31.0 %copy-start.1 = (bf16[768,256]{1,0:T(8,128)(2,1)}, bf16[768,256]{1,0:T(8,128)(2,1)S(1)}, u32[]{:S(2)}) copy-start(bf16[768,256]{1,0:T(8,128)(2,1)S(1)} %squeeze.25) | copy-start | bytes 1179652
  250.5 8.4 %collective-permute-start.1 = (f32[256,256]{1,0:T(8,128)S(1)}, f32[256,256]{1,0:T(8,128)S(1)}, u32[]{:S(2)}, u32[]{:S(2)}) collective-permute-start(f32[256,256]{1,0:T(8,128)S(1)} %add.118), channel_id=1, source_target_pairs={{0,16},{1,17},{2,18},{3,19},{4,20},{5,21},{6,22},{7,23},{8,24},{9,... | collective-permute-start | bytes 786440 | tf_op jit(solution)/shard_map/ppermute | solution.py:25
  255.8 23.1 %copy-start.5 = (bf16[768,768]{1,0:T(8,128)(2,1)}, bf16[768,768]{1,0:T(8,128)(2,1)S(1)}, u32[]{:S(2)}) copy-start(bf16[768,768]{1,0:T(8,128)(2,1)S(1)} %select_convert_fusion.1) | copy-start | bytes 3538948
  259.6 17.7 %collective-permute-start.2 = (f32[256,256]{1,0:T(8,128)}, f32[256,256]{1,0:T(8,128)}, u32[]{:S(2)}, u32[]{:S(2)}) collective-permute-start(f32[256,256]{1,0:T(8,128)} %add.119), channel_id=1, source_target_pairs={{0,32},{1,33},{2,34},{3,35},{4,36},{5,37},{6,38},{7,39},{8,40},{9,... | collective-permute-start | bytes 786440 | tf_op jit(solution)/shard_map/ppermute | solution.py:25
  279.9 177.4 %copy-start.10 = (bf16[768,256]{1,0:T(8,128)(2,1)S(1)}, bf16[768,256]{1,0:T(8,128)(2,1)}, u32[]{:S(2)}) copy-start(bf16[768,256]{1,0:T(8,128)(2,1)} %squeeze.27) | copy-start | bytes 1179652
  280.3 189.8 %copy-start.3 = (bf16[768,256]{0,1:T(8,128)(2,1)}, bf16[768,256]{0,1:T(8,128)(2,1)S(1)}, u32[]{:S(2)}) copy-start(bf16[768,256]{0,1:T(8,128)(2,1)S(1)} %multiply_convert_fusion) | copy-start | bytes 1179652
  281.3 188.3 %copy-start.12 = (bf16[768,256]{1,0:T(8,128)(2,1)S(1)}, bf16[768,256]{1,0:T(8,128)(2,1)}, u32[]{:S(2)}) copy-start(bf16[768,256]{1,0:T(8,128)(2,1)} %squeeze.26) | copy-start | bytes 1179652
  344.0 112.0 %all-reduce.5.cloned.1.call-start = ((), (), s32[]{:S(2)}) async-start(), calls=%async_computation.9 | async-start | bytes 524288 | tf_op jit(solution)/shard_map/psum | solution.py:39
  344.5 125.5 %copy-start.17 = (bf16[256,256]{1,0:T(8,128)(2,1)S(1)}, bf16[256,256]{1,0:T(8,128)(2,1)}, u32[]{:S(2)}) copy-start(bf16[256,256]{1,0:T(8,128)(2,1)} %copy-done.16) | copy-start | bytes 393220
  455.9 11.5 %collective-permute-start.3 = (f32[256,256]{0,1:T(8,128)}, f32[256,256]{0,1:T(8,128)S(1)}, u32[]{:S(2)}, u32[]{:S(2)}) collective-permute-start(f32[256,256]{0,1:T(8,128)} %all-reduce.5.cloned.1.call-done), channel_id=1, source_target_pairs={{8,0},{9,1},{10,2},{11,3},{12,4},{13,5},{14,6},{15,7},{16,8},{17,9... | collective-permute-start | bytes 786440 | tf_op jit(solution)/shard_map/ppermute | solution.py:25
  457.9 12.5 %copy-start.7 = (bf16[768,768]{1,0:T(8,128)(2,1)}, bf16[768,768]{1,0:T(8,128)(2,1)S(1)}, u32[]{:S(2)}) copy-start(bf16[768,768]{1,0:T(8,128)(2,1)S(1)} %select_convert_fusion) | copy-start | bytes 3538948
  468.1 36.4 %collective-permute-start.4 = (f32[256,256]{0,1:T(8,128)}, f32[256,256]{0,1:T(8,128)}, u32[]{:S(2)}, u32[]{:S(2)}) collective-permute-start(f32[256,256]{0,1:T(8,128)} %add.129), channel_id=1, source_target_pairs={{16,0},{17,1},{18,2},{19,3},{20,4},{21,5},{22,6},{23,7},{24,8},{25... | collective-permute-start | bytes 786440 | tf_op jit(solution)/shard_map/ppermute | solution.py:25
  475.6 49.7 %all-to-all-start.5 = ((bf16[64,2,1536]{2,1,0:T(2,128)(2,1)}), bf16[64,2,1536]{2,1,0:T(2,128)(2,1)}, u32[]{:S(2)}, u32[]{:S(2)}) async-start(bf16[64,2,1536]{2,1,0:T(2,128)(2,1)} %reshape.94), calls=%async_computation.5 | async-start | bytes 786432 | tf_op jit(solution)/shard_map/all_to_all | solution.py:101
  505.6 13.4 %copy-start.20 = (f32[256,256]{0,1:T(8,128)S(1)}, f32[256,256]{0,1:T(8,128)}, u32[]{:S(2)}) copy-start(f32[256,256]{0,1:T(8,128)} %all-reduce.5.cloned.1.call-done) | copy-start | bytes 786436
  505.6 13.4 %collective-permute-start.5 = (f32[256,256]{0,1:T(8,128)S(1)}, f32[256,256]{0,1:T(8,128)S(1)}, u32[]{:S(2)}, u32[]{:S(2)}) collective-permute-start(f32[256,256]{0,1:T(8,128)S(1)} %add.130), channel_id=1, source_target_pairs={{32,0},{33,1},{34,2},{35,3},{36,4},{37,5},{38,6},{39,7},{40,8},{41... | collective-permute-start | bytes 786440 | tf_op jit(solution)/shard_map/ppermute | solution.py:25
  520.7 16.7 %copy-start.11 = (bf16[768,256]{1,0:T(8,128)(2,1)S(1)}, bf16[768,256]{1,0:T(8,128)(2,1)}, u32[]{:S(2)}) copy-start(bf16[768,256]{1,0:T(8,128)(2,1)} %squeeze.27) | copy-start | bytes 1179652
  520.7 17.0 %copy-start.2 = (bf16[768,256]{1,0:T(8,128)(2,1)S(1)}, bf16[768,256]{1,0:T(8,128)(2,1)}, u32[]{:S(2)}) copy-start(bf16[768,256]{1,0:T(8,128)(2,1)} %copy-done.1) | copy-start | bytes 1179652
  520.7 17.0 %copy-start.8 = (bf16[768,768]{1,0:T(8,128)(2,1)S(1)}, bf16[768,768]{1,0:T(8,128)(2,1)}, u32[]{:S(2)}) copy-start(bf16[768,768]{1,0:T(8,128)(2,1)} %copy-done.7) | copy-start | bytes 3538948
  525.3 26.6 %all-to-all-start.7 = ((bf16[64,2,1536]{2,1,0:T(2,128)(2,1)}), bf16[64,2,1536]{2,1,0:T(2,128)(2,1)S(1)}, u32[]{:S(2)}, u32[]{:S(2)}) async-start(bf16[64,2,1536]{2,1,0:T(2,128)(2,1)} %reshape.98), calls=%async_computation.7 | async-start | bytes 786432 | tf_op jit(solution)/shard_map/all_to_all | solution.py:103
  552.0 20.8 %all-to-all-start.6 = ((bf16[64,2,1536]{2,1,0:T(2,128)(2,1)}), bf16[64,2,1536]{2,1,0:T(2,128)(2,1)S(1)}, u32[]{:S(2)}, u32[]{:S(2)}) async-start(bf16[64,2,1536]{2,1,0:T(2,128)(2,1)} %reshape.96), calls=%async_computation.6 | async-start | bytes 786432 | tf_op jit(solution)/shard_map/all_to_all | solution.py:102
  (9 other events, 42.3 us)
Sparse Core Ops, SparseCore 0:
  66.7 57.0 all-gather.4
  127.5 108.3 all-reduce.2
  281.4 62.4 all-gather.6
  347.5 108.3 all-reduce.4
where the time goes:
time: 585 us; the launch traced here: 583 us
  waiting for transfers between devices  365 us (62%)
  starting transfers between devices  98.4 us (17%)
  other arithmetic  37.9 us (6%)
  local copies, waits for them, and re-layouts  36.2 us (6%)
  blocking collectives  23.5 us (4%)
  between operations  14.5 us (2%)
  matrix products  7.42 us (1%)
    psum x2, waiting for transfers between devices, carry_states(): total = lax.psum(state, 'ctx')  223 us
    all_gather x2, waiting for transfers between devices, entering(): pieces = lax.all_gather(value, axis)  65.1 us
    all_to_all x1, starting transfers between devices, local(): lax.all_to_all(grad_q.astype(bf16)[None], 'head', split_axis=1, concat_ax...  24.5 us
    all_to_all x1, blocking collectives, local(): lax.all_to_all(by_part(values), 'head', split_axis=0, concat_axis=1, tile...  23.5 us
    select_n x22, other arithmetic, step(): return jnp.where(position < mine, longer, subtotal)  23 us
    ppermute x6, starting transfers between devices, shifted(): return lax.ppermute(block, axis, route)  21.9 us
    all_to_all x1, waiting for transfers between devices, local(): lax.all_to_all(by_part(out_grad), 'head', split_axis=0, concat_axis=1, ti...  16.3 us
    all_to_all x1, waiting for transfers between devices, local(): lax.all_to_all(by_part(gates), 'head', split_axis=0, concat_axis=1, tiled...  16.2 us
  transfers between devices with their start and end apart: 17, of which 11 were waited for; matrix products, arithmetic and copies ran while one was open for 11% of the time, Pallas kernels for 0%

commit v1 on v0

v1 whole, which is shorter than its diff:
```python
import jax
import jax.numpy as jnp
from jax import lax
from jax.experimental import pallas as pl
from jax.experimental.pallas import tpu as pltpu
from jax.sharding import PartitionSpec as P

F32 = jnp.float32
BF16 = jnp.bfloat16


def exchange(x, axes, groups=None):
    return lax.all_to_all(x, axes, 0, 0, axis_index_groups=groups, tiled=True)


def scan_kernel(reverse, blocks, in_ref, out_ref):
    running = jnp.zeros(in_ref.shape[1:], F32)
    for position in range(blocks):
        block = blocks - 1 - position if reverse else position
        out_ref[block] = running.astype(BF16)
        running = running + in_ref[block].astype(F32)


def exclusive_sum(pieces, reverse):
    blocks = pieces.shape[0]

    def body(in_ref, out_ref):
        scan_kernel(reverse, blocks, in_ref, out_ref)

    return pl.pallas_call(
        body,
        out_shape=jax.ShapeDtypeStruct(pieces.shape, BF16),
        in_specs=[pl.BlockSpec(memory_space=pltpu.VMEM)],
        out_specs=pl.BlockSpec(memory_space=pltpu.VMEM),
    )(pieces)


def carry_states(state, reverse, groups):
    rows, cols = state.shape
    tiles = state.astype(BF16).reshape(rows // 8, 8, cols // 128, 128).transpose(0, 2, 1, 3)
    tiles = jnp.pad(tiles, ((0, 0), (0, 1), (0, 0), (0, 0))).reshape(96, 8, 128)
    gathered = exchange(tiles, ("ctx", "head"), groups)
    summed = exclusive_sum(gathered, reverse)
    back = exchange(summed, ("ctx", "head"), groups).reshape(rows // 8, 3, 8, 128)
    return back[:, :2].transpose(0, 2, 1, 3).reshape(rows, cols)


def local(queries, keys, values, gates, out_grad, gains):
    split, heads, _, _, piece, dh = queries.shape
    shape = queries.shape
    n_ctx = lax.axis_size("ctx")
    n_head = lax.axis_size("head")
    xs, cores = n_head // (heads * 2), 2
    groups = [
        [c * n_head + ((p // 2) * heads + h) * 2 + p % 2 for p in range(split) for c in range(n_ctx)]
        for h in range(heads)
    ]

    def to_pieces(array):
        return array.reshape(xs, cores, heads, piece, dh).transpose(0, 2, 1, 3, 4).reshape(n_head, piece, dh)

    gate = gates.astype(F32)
    dnorm = out_grad.astype(F32) * gains[None, :, None, None, None, :] * jax.nn.silu(gate)
    sent = jnp.concatenate(
        [to_pieces(queries), to_pieces(keys), to_pieces(values), to_pieces(dnorm.astype(BF16))], axis=1
    )
    got = exchange(sent, "head")
    q, k, v, d = (got[:, n * piece : (n + 1) * piece].reshape(n_head * piece, dh) for n in range(4))
    rows = q.shape[0]
    causal = jnp.arange(rows)[:, None] >= jnp.arange(rows)[None, :]
    state = jnp.einsum("se,sf->ef", k, v, preferred_element_type=F32)
    carried = carry_states(state, False, groups)
    scores = jnp.einsum("te,se->ts", q, k, preferred_element_type=F32)
    masked = jnp.where(causal, scores, 0.0).astype(BF16)
    mixed = jnp.dot(q, carried, preferred_element_type=F32) + jnp.dot(masked, v, preferred_element_type=F32)
    inv = lax.rsqrt(jnp.mean(mixed * mixed, -1, keepdims=True) + 1e-05)
    normed = mixed * inv
    dnormed = d.astype(F32)
    dmixed = (inv * (dnormed - normed * jnp.mean(dnormed * normed, -1, keepdims=True))).astype(BF16)
    back_state = jnp.einsum("te,tf->ef", q, dmixed, preferred_element_type=F32)
    later = carry_states(back_state, True, groups)
    across = jnp.einsum("tf,sf->ts", dmixed, v, preferred_element_type=F32)
    across = jnp.where(causal, across, 0.0).astype(BF16)
    grad_q = jnp.einsum("tf,ef->te", dmixed, carried, preferred_element_type=F32) + jnp.dot(
        across, k, preferred_element_type=F32
    )
    grad_k = jnp.einsum("sf,ef->se", v, later, preferred_element_type=F32) + jnp.einsum(
        "ts,te->se", across, q, preferred_element_type=F32
    )
    grad_v = jnp.dot(k, later, preferred_element_type=F32) + jnp.einsum(
        "ts,tf->sf", masked, dmixed, preferred_element_type=F32
    )
    grads = jnp.concatenate([g.astype(BF16).reshape(n_head, piece, dh) for g in (grad_q, grad_k, grad_v)], axis=1)
    back = exchange(grads, "head").reshape(xs, heads, cores, 3 * piece, dh).transpose(0, 2, 1, 3, 4)
    return tuple(back[:, :, :, n * piece : (n + 1) * piece].reshape(shape) for n in range(3))


def solution(mesh):
    placed = P(None, None, "ctx", "head", None, None)
    return jax.shard_map(
        local,
        mesh=mesh,
        in_specs=(placed,) * 5 + (P(),),
        out_specs=(placed,) * 3,
        check_vma=False,
    )
```

time: 585 us -> 210 us (0.36)
  waiting for transfers between devices: 365 us -> 24.5 us
  blocking collectives: 23.5 us -> 147 us
  starting transfers between devices: 98.4 us -> 11.9 us
  other arithmetic: 37.9 us -> 3.25 us
  local copies, waits for them, and re-layouts: 36.2 us -> 6.12 us
  between operations: 14.5 us -> 0.9 us
    psum x2 -> x0, waiting for transfers between devices: 223 us -> none  [carry_states(): total = lax.psum(state, 'ctx')]
    all_to_all x1 -> x4, blocking collectives: 23.5 us -> 147 us  [exchange(): return lax.all_to_all(x, axes, 0, 0, axis_index_groups=groups, tiled=True)]
    all_gather x2 -> x0, waiting for transfers between devices: 65.1 us -> none  [entering(): pieces = lax.all_gather(value, axis)]
    all_to_all x7 -> x2, starting transfers between devices: 76.4 us -> 11.9 us  [exchange(): return lax.all_to_all(x, axes, 0, 0, axis_index_groups=groups, tiled=True)]
    all_to_all x7 -> x2, waiting for transfers between devices: 62.8 us -> 24.5 us  [exchange(): return lax.all_to_all(x, axes, 0, 0, axis_index_groups=groups, tiled=True)]
    select_n x22 -> x0, other arithmetic: 23 us -> none  [step(): return jnp.where(position < mine, longer, subtotal)]
    ppermute x6 -> x0, starting transfers between devices: 21.9 us -> none  [shifted(): return lax.ppermute(block, axis, route)]
    unnamed x63 -> x6, local copies, waits for them, and re-layouts: 14.1 us -> 0.66 us
  transfers between devices with their start and end apart: 17 -> 2, of which waited for: 11 -> 2; matrix products, arithmetic and copies ran while one was open for 11% -> 4% of each run, Pallas kernels for 0% -> 0%
where the time goes in v1:
time: 210 us
  blocking collectives  147 us (70%)
  waiting for transfers between devices  24.5 us (12%)
  matrix products  12.3 us (6%)
  starting transfers between devices  11.9 us (6%)
  local copies, waits for them, and re-layouts  6.12 us (3%)
  Pallas kernels  3.41 us (2%)
  other arithmetic  3.25 us (2%)
    all_to_all x4, blocking collectives, exchange(): return lax.all_to_all(x, axes, 0, 0, axis_index_groups=groups, tiled=True)  147 us
    all_to_all x2, waiting for transfers between devices, exchange(): return lax.all_to_all(x, axes, 0, 0, axis_index_groups=groups, tiled=True)  24.5 us
    all_to_all x2, starting transfers between devices, exchange(): return lax.all_to_all(x, axes, 0, 0, axis_index_groups=groups, tiled=True)  11.9 us
  transfers between devices with their start and end apart: 2, of which 2 were waited for; matrix products, arithmetic and copies ran while one was open for 4% of the time, Pallas kernels for 0%

profile of v1, /device:TPU:1, one launch (start us, length us, event | category | flops | bytes accessed | tf_op | source)
XLA Modules:
  0.0 209.7 jit_solution(16992094861196761855)
XLA Ops:
  0.7 1.4 fusion.10
  2.5 0.6 copy-done.2
  3.2 0.6 pad_maximum_fusion
  3.9 53.6 %all_to_all.30 = bf16[64,48,256]{2,1,0:T(8,128)(2,1)S(1)} all-to-all(bf16[64,48,256]{2,1,0:T(8,128)(2,1)S(1)} %pad_maximum_fusion), channel_id=1, replica_groups=mesh['ctx'=12,'head'=64] {'head'}, dimensions={0} | all-to-all | bytes 3145728 | tf_op jit(solution)/shard_map/all_to_all | solution.py:13
  57.5 0.5 fusion.17
  58.0 0.4 fusion.4
  58.4 32.3 %all_to_all.31.in_ref = bf16[96,8,128]{2,1,0:T(8,128)(2,1)} all-to-all(bf16[96,8,128]{2,1,0:T(8,128)(2,1)S(1)} %bitcast.79), channel_id=1, replica_groups={{0,64,128,192,256,320,384,448,512,576,640,704,1,65,129,193,257,321,385,..., dimensions={0} | all-to-all | bytes 393216 | tf_op jit(solution)/shard_map/all_to_all | solution.py:13
  90.7 1.7 shard_map.85
  92.4 6.3 %all-to-all-start.2 = ((bf16[96,8,128]{2,1,0:T(8,128)(2,1)}), bf16[96,8,128]{2,1,0:T(8,128)(2,1)}, u32[]{:S(2)}, u32[]{:S(2)}) async-start(bf16[96,8,128]{2,1,0:T(8,128)(2,1)} %shard_map.85), calls=%async_computation.2 | async-start | bytes 393216 | tf_op jit(solution)/shard_map/all_to_all | solution.py:13
  99.2 0.3 copy.36
  99.4 0.5 select_convert_fusion.1
  99.9 14.7 %all-to-all-done.2 = bf16[96,8,128]{2,1,0:T(8,128)(2,1)} async-done(((bf16[96,8,128]{2,1,0:T(8,128)(2,1)}), bf16[96,8,128]{2,1,0:T(8,128)(2,1)}, u32[]{:S(2)}, u32[]{:S(2)}) %all-to-all-start.2) | async-done | bytes 196640 | tf_op jit(solution)/shard_map/all_to_all | solution.py:13
  114.7 1.2 fusion.14
  115.9 0.5 multiply_reduce_fusion.1
  116.7 0.3 fusion.5
  117.1 21.6 %all_to_all.32.in_ref = bf16[96,8,128]{2,1,0:T(8,128)(2,1)} all-to-all(bf16[96,8,128]{2,1,0:T(8,128)(2,1)S(1)} %bitcast.78), channel_id=1, replica_groups={{0,64,128,192,256,320,384,448,512,576,640,704,1,65,129,193,257,321,385,..., dimensions={0} | all-to-all | bytes 393216 | tf_op jit(solution)/shard_map/all_to_all | solution.py:13
  138.7 1.7 shard_map.86
  140.4 5.6 %all-to-all-start.4 = ((bf16[96,8,128]{2,1,0:T(8,128)(2,1)}), bf16[96,8,128]{2,1,0:T(8,128)(2,1)S(1)}, u32[]{:S(2)}, u32[]{:S(2)}) async-start(bf16[96,8,128]{2,1,0:T(8,128)(2,1)} %shard_map.86), calls=%async_computation.4 | async-start | bytes 393216 | tf_op jit(solution)/shard_map/all_to_all | solution.py:13
  146.0 1.2 fusion.13
  147.2 1.5 select_convert_fusion
  148.7 2.5 %fusion = bf16[768,256]{1,0:T(8,128)(2,1)} fusion(f32[768,256]{1,0:T(8,128)S(1)} %fusion.13, bf16[768,768]{1,0:T(8,128)(2,1)} %select_convert_fusion, bf16[768,256]{1,0:T(8,128)(2,1)S(1)} %reshape.115), kind=kOutput, calls=%fused_computation.9 | convolution fusion | flops 302383104 | bytes 2752512 | tf_op jit(solution)/shard_map/dot_general | solution.py:84
  151.2 1.1 reshape.117
  152.3 9.8 %all-to-all-done.4 = bf16[96,8,128]{2,1,0:T(8,128)(2,1)S(1)} async-done(((bf16[96,8,128]{2,1,0:T(8,128)(2,1)}), bf16[96,8,128]{2,1,0:T(8,128)(2,1)S(1)}, u32[]{:S(2)}, u32[]{:S(2)}) %all-to-all-start.4) | async-done | bytes 196640 | tf_op jit(solution)/shard_map/all_to_all | solution.py:13
  162.1 0.3 fusion.15
  162.4 1.2 fusion.16
  163.6 0.5 fusion.2
  164.2 2.0 fusion.1
  166.3 0.4 pad_maximum_fusion.1
  166.8 39.8 %all_to_all.33 = bf16[64,36,256]{2,1,0:T(8,128)(2,1)S(1)} all-to-all(bf16[64,36,256]{2,1,0:T(8,128)(2,1)S(1)} %pad_maximum_fusion.1), channel_id=1, replica_groups=mesh['ctx'=12,'head'=64] {'head'}, dimensions={0} | all-to-all | bytes 2359296 | tf_op jit(solution)/shard_map/all_to_all | solution.py:13
  206.8 1.0 copy.37
  207.7 1.0 copy.38
  208.7 1.0 copy.39
  (22 shorter events, 1.5 us)
Async XLA Ops:
  0.6 1.6 copy-start
  0.6 1.7 copy-start.1
  2.1 1.0 copy-start.2
  92.4 22.2 %all-to-all-start.2 = ((bf16[96,8,128]{2,1,0:T(8,128)(2,1)}), bf16[96,8,128]{2,1,0:T(8,128)(2,1)}, u32[]{:S(2)}, u32[]{:S(2)}) async-start(bf16[96,8,128]{2,1,0:T(8,128)(2,1)} %shard_map.85), calls=%async_computation.2 | async-start | bytes 393216 | tf_op jit(solution)/shard_map/all_to_all | solution.py:13
  140.4 21.7 %all-to-all-start.4 = ((bf16[96,8,128]{2,1,0:T(8,128)(2,1)}), bf16[96,8,128]{2,1,0:T(8,128)(2,1)S(1)}, u32[]{:S(2)}, u32[]{:S(2)}) async-start(bf16[96,8,128]{2,1,0:T(8,128)(2,1)} %shard_map.86), calls=%async_computation.4 | async-start | bytes 393216 | tf_op jit(solution)/shard_map/all_to_all | solution.py:13

commit v2 on v1

v2 whole, which is shorter than its diff:
```python
import jax
import jax.numpy as jnp
from jax import lax
from jax.sharding import PartitionSpec as P

F32 = jnp.float32
BF16 = jnp.bfloat16


def exchange(x, axes, groups=None):
    return lax.all_to_all(x, axes, 0, 0, axis_index_groups=groups, tiled=True)


def to_pieces(state, n):
    rows, cols = state.shape
    tiles = -(-rows * cols // (8 * 128 * n)) * n
    high = tiles * 128 // cols * 8
    full = jnp.pad(state.astype(BF16), ((0, high - rows), (0, 0)))
    full = full.reshape(high // 8, 8, cols // 128, 128).transpose(0, 2, 1, 3)
    return full.reshape(n, tiles // n, 8, 128).transpose(0, 2, 1, 3).reshape(n, 8, tiles // n * 128)


def from_pieces(pieces, rows, cols):
    n, _, width = pieces.shape
    full = pieces.reshape(n, 8, width // 128, 128).transpose(0, 2, 1, 3)
    full = full.reshape(-1, cols // 128, 8, 128).transpose(0, 2, 1, 3).reshape(-1, cols)
    return full[:rows]


def carry_states(state, rest, meanwhile, reverse, wanted, groups):
    rows, cols = state.shape
    n_ctx = lax.axis_size("ctx")
    split = len(groups[0])
    at = jnp.arange(n_ctx)
    order = (at[:, None] < at[None, :] if reverse else at[:, None] > at[None, :]).astype(BF16)
    pieces, rest = lax.optimization_barrier((to_pieces(state, n_ctx), rest))
    pieces = exchange(pieces, "ctx")
    total = jnp.sum(pieces.astype(F32), 0)
    sent = jnp.broadcast_to(total.astype(BF16)[None], (split,) + total.shape)
    sent, rest = lax.optimization_barrier((sent, rest))
    totals = exchange(sent, "head", groups)
    done = meanwhile(*rest)
    inside = jnp.einsum("ab,brl->arl", order, pieces, preferred_element_type=F32)
    outside = jnp.sum(totals.astype(F32) * wanted[:, None, None], 0)
    back, done = lax.optimization_barrier(((inside + outside[None]).astype(BF16), done))
    back, done = lax.optimization_barrier((exchange(back, "ctx"), done))
    return from_pieces(back, rows, cols), done


def local(queries, keys, values, gates, out_grad, gains):
    split, heads, _, _, piece, dh = queries.shape
    shape = queries.shape
    n_head = lax.axis_size("head")
    xs, cores = n_head // (heads * 2), 2
    groups = [[((p // 2) * heads + h) * 2 + p % 2 for p in range(split)] for h in range(heads)]
    me = lax.axis_index("head")
    row = me // (heads * 2) * 2 + me % 2
    other = jnp.arange(split)
    before, after = ((other < row).astype(F32), (other > row).astype(F32))

    def for_devices(array):
        return array.reshape(xs, cores, heads, piece, dh).transpose(0, 2, 1, 3, 4).reshape(n_head, piece, dh)

    gate = gates.astype(F32)
    dnorm = out_grad.astype(F32) * gains[None, :, None, None, None, :] * jax.nn.silu(gate)
    sent = jnp.concatenate(
        [for_devices(queries), for_devices(keys), for_devices(values), for_devices(dnorm.astype(BF16))], axis=1
    )
    sent, before, after = lax.optimization_barrier((sent, before, after))
    got = exchange(sent, "head")
    q, k, v, d = (got[:, n * piece : (n + 1) * piece].reshape(n_head * piece, dh) for n in range(4))
    rows = q.shape[0]
    causal = jnp.arange(rows)[:, None] >= jnp.arange(rows)[None, :]
    state = jnp.einsum("se,sf->ef", k, v, preferred_element_type=F32)

    def inner(q, k, v, d):
        scores = jnp.einsum("te,se->ts", q, k, preferred_element_type=F32)
        masked = jnp.where(causal, scores, 0.0).astype(BF16)
        return q, k, v, d, masked

    carried, (q, k, v, d, masked) = carry_states(state, (q, k, v, d), inner, False, before, groups)
    mixed = jnp.dot(q, carried, preferred_element_type=F32) + jnp.dot(masked, v, preferred_element_type=F32)
    inv = lax.rsqrt(jnp.mean(mixed * mixed, -1, keepdims=True) + 1e-05)
    normed = mixed * inv
    dnormed = d.astype(F32)
    dmixed = (inv * (dnormed - normed * jnp.mean(dnormed * normed, -1, keepdims=True))).astype(BF16)
    back_state = jnp.einsum("te,tf->ef", q, dmixed, preferred_element_type=F32)

    def inner_back(q, k, v, masked, dmixed, carried):
        within_v = jnp.einsum("ts,tf->sf", masked, dmixed, preferred_element_type=F32)
        across = jnp.einsum("tf,sf->ts", dmixed, v, preferred_element_type=F32)
        across = jnp.where(causal, across, 0.0).astype(BF16)
        grad_q = jnp.einsum("tf,ef->te", dmixed, carried, preferred_element_type=F32) + jnp.dot(
            across, k, preferred_element_type=F32
        )
        within_k = jnp.einsum("ts,te->se", across, q, preferred_element_type=F32)
        return k, v, grad_q.astype(BF16), within_k, within_v

    later, (k, v, grad_q, within_k, within_v) = carry_states(
        back_state, (q, k, v, masked, dmixed, carried), inner_back, True, after, groups
    )
    grad_k = jnp.einsum("sf,ef->se", v, later, preferred_element_type=F32) + within_k
    grad_v = jnp.dot(k, later, preferred_element_type=F32) + within_v
    grads = jnp.concatenate([g.astype(BF16).reshape(n_head, piece, dh) for g in (grad_q, grad_k, grad_v)], axis=1)
    back = exchange(grads, "head").reshape(xs, heads, cores, 3 * piece, dh).transpose(0, 2, 1, 3, 4)
    return tuple(back[:, :, :, n * piece : (n + 1) * piece].reshape(shape) for n in range(3))


def solution(mesh):
    placed = P(None, None, "ctx", "head", None, None)
    return jax.shard_map(
        local,
        mesh=mesh,
        in_specs=(placed,) * 5 + (P(),),
        out_specs=(placed,) * 3,
        check_vma=False,
    )
```

time: 210 us -> 197 us (0.938)
  waiting for transfers between devices: 24.5 us -> 6.23 us
  blocking collectives: 147 us -> 161 us
  matrix products: 12.3 us -> 6.25 us
  Pallas kernels: 3.41 us -> 0 us
    all_to_all x2, waiting for transfers between devices: 24.5 us -> 6.23 us  [exchange(): return lax.all_to_all(x, axes, 0, 0, axis_index_groups=groups, tiled=True)]
    all_to_all x4 -> x6, blocking collectives: 147 us -> 161 us  [exchange(): return lax.all_to_all(x, axes, 0, 0, axis_index_groups=groups, tiled=True)]
    dot_general x8 -> x10, matrix products: 9.77 us -> 4.66 us  [the longest x1 1.39 us: inner_back(): jnp.einsum('ts,tf->sf', masked, dmixed, preferred_element_type=F32)]
    pallas_call x2 -> x0, Pallas kernels: 3.41 us -> none  [exclusive_sum(): pl.pallas_call(body, out_shape=jax.ShapeDtypeStruct(pieces.shape, BF16),...]
  transfers between devices with their start and end apart: 2 -> 2, of which waited for: 2 -> 2; matrix products, arithmetic and copies ran while one was open for 4% -> 2% of each run, Pallas kernels for 0% -> 0%
where the time goes in v2:
time: 197 us; the launch traced here: 196 us
  blocking collectives  161 us (82%)
  starting transfers between devices  12.1 us (6%)
  local copies, waits for them, and re-layouts  6.96 us (4%)
  matrix products  6.25 us (3%)
  waiting for transfers between devices  6.23 us (3%)
  other arithmetic  3.02 us (2%)
    all_to_all x6, blocking collectives, exchange(): return lax.all_to_all(x, axes, 0, 0, axis_index_groups=groups, tiled=True)  161 us
    all_to_all x2, starting transfers between devices, exchange(): return lax.all_to_all(x, axes, 0, 0, axis_index_groups=groups, tiled=True)  12.1 us
    all_to_all x2, waiting for transfers between devices, exchange(): return lax.all_to_all(x, axes, 0, 0, axis_index_groups=groups, tiled=True)  6.23 us
  transfers between devices with their start and end apart: 2, of which 2 were waited for; matrix products, arithmetic and copies ran while one was open for 2% of the time, Pallas kernels for 0%

profile of v2, /device:TPU:1, one launch (start us, length us, event | category | flops | bytes accessed | tf_op | source)
XLA Modules:
  0.0 196.5 jit_solution(2446435663527434432)
XLA Ops:
  0.7 1.4 fusion.13
  2.5 0.6 copy-done.3
  3.2 0.6 pad_maximum_fusion
  3.9 53.6 %all_to_all.40 = bf16[64,48,256]{2,1,0:T(8,128)(2,1)S(1)} all-to-all(bf16[64,48,256]{2,1,0:T(8,128)(2,1)S(1)} %pad_maximum_fusion), channel_id=1, replica_groups=mesh['ctx'=12,'head'=64] {'head'}, dimensions={0} | all-to-all | bytes 3145728 | tf_op jit(solution)/shard_map/all_to_all | solution.py:11
  57.5 0.5 fusion.23
  58.1 0.4 fusion.5
  58.9 23.6 %all_to_all.41 = bf16[12,8,768]{2,1,0:T(8,128)(2,1)S(1)} all-to-all(bf16[12,8,768]{2,1,0:T(8,128)(2,1)S(1)} %bitcast.100), channel_id=1, replica_groups=mesh['ctx'=12,'head'=64] {'ctx'}, dimensions={0} | all-to-all | bytes 294912 | tf_op jit(solution)/shard_map/all_to_all | solution.py:11
  82.5 0.7 broadcast_in_dim.8
  83.1 5.7 %all-to-all-start.2 = ((bf16[8,8,768]{2,1,0:T(8,128)(2,1)}), bf16[8,8,768]{2,1,0:T(8,128)(2,1)S(1)}, u32[]{:S(2)}, u32[]{:S(2)}) async-start(bf16[8,8,768]{2,1,0:T(8,128)(2,1)} %broadcast_in_dim.8), calls=%async_computation.2 | async-start | bytes 196608 | tf_op jit(solution)/shard_map/all_to_all | solution.py:11
  88.9 0.5 select_convert_fusion.1
  89.4 4.5 %all-to-all-done.2 = bf16[8,8,768]{2,1,0:T(8,128)(2,1)S(1)} async-done(((bf16[8,8,768]{2,1,0:T(8,128)(2,1)}), bf16[8,8,768]{2,1,0:T(8,128)(2,1)S(1)}, u32[]{:S(2)}, u32[]{:S(2)}) %all-to-all-start.2) | async-done | bytes 98336 | tf_op jit(solution)/shard_map/all_to_all | solution.py:11
  94.2 13.5 %all_to_all.42 = bf16[12,8,768]{2,1,0:T(8,128)(2,1)S(1)} all-to-all(bf16[12,8,768]{2,1,0:T(8,128)(2,1)S(1)} %copy.57), channel_id=1, replica_groups=mesh['ctx'=12,'head'=64] {'ctx'}, dimensions={0} | all-to-all | bytes 294912 | tf_op jit(solution)/shard_map/all_to_all | solution.py:11
  107.9 0.3 fusion.22
  108.2 0.5 multiply_reduce_fusion
  109.1 0.3 convolution_convert_fusion
  109.4 14.6 %all_to_all.43 = bf16[12,8,768]{2,1,0:T(8,128)(2,1)S(1)} all-to-all(bf16[12,8,768]{2,1,0:T(8,128)(2,1)S(1)} %bitcast.101), channel_id=1, replica_groups=mesh['ctx'=12,'head'=64] {'ctx'}, dimensions={0} | all-to-all | bytes 294912 | tf_op jit(solution)/shard_map/all_to_all | solution.py:11
  124.0 0.7 broadcast_in_dim.11
  124.7 6.4 %all-to-all-start.5 = ((bf16[8,8,768]{2,1,0:T(8,128)(2,1)}), bf16[8,8,768]{2,1,0:T(8,128)(2,1)S(1)}, u32[]{:S(2)}, u32[]{:S(2)}) async-start(bf16[8,8,768]{2,1,0:T(8,128)(2,1)} %broadcast_in_dim.11), calls=%async_computation.5 | async-start | bytes 196608 | tf_op jit(solution)/shard_map/all_to_all | solution.py:11
  131.0 0.3 fusion.25
  131.4 1.4 fusion.27
  132.7 0.5 select_convert_fusion
  133.3 0.5 fusion
  133.8 0.5 fusion.26
  134.3 1.7 all-to-all-done.5
  136.4 13.9 %all_to_all.44 = bf16[12,8,768]{2,1,0:T(8,128)(2,1)S(1)} all-to-all(bf16[12,8,768]{2,1,0:T(8,128)(2,1)S(1)} %copy.60), channel_id=1, replica_groups=mesh['ctx'=12,'head'=64] {'ctx'}, dimensions={0} | all-to-all | bytes 294912 | tf_op jit(solution)/shard_map/all_to_all | solution.py:11
  150.4 0.3 fusion.2
  150.8 0.3 fusion.1
  151.2 0.4 pad_maximum_fusion.1
  151.6 41.7 %all_to_all.45 = bf16[64,36,256]{2,1,0:T(8,128)(2,1)S(1)} all-to-all(bf16[64,36,256]{2,1,0:T(8,128)(2,1)S(1)} %pad_maximum_fusion.1), channel_id=1, replica_groups=mesh['ctx'=12,'head'=64] {'head'}, dimensions={0} | all-to-all | bytes 2359296 | tf_op jit(solution)/shard_map/all_to_all | solution.py:11
  193.5 1.0 copy.63
  194.5 1.0 copy.62
  195.5 1.0 copy.61
  (36 shorter events, 2.5 us)
Async XLA Ops:
  0.6 1.6 copy-start.1
  0.6 1.7 copy-start.2
  2.1 1.0 copy-start.3
  83.1 10.7 %all-to-all-start.2 = ((bf16[8,8,768]{2,1,0:T(8,128)(2,1)}), bf16[8,8,768]{2,1,0:T(8,128)(2,1)S(1)}, u32[]{:S(2)}, u32[]{:S(2)}) async-start(bf16[8,8,768]{2,1,0:T(8,128)(2,1)} %broadcast_in_dim.8), calls=%async_computation.2 | async-start | bytes 196608 | tf_op jit(solution)/shard_map/all_to_all | solution.py:11
  124.7 11.4 %all-to-all-start.5 = ((bf16[8,8,768]{2,1,0:T(8,128)(2,1)}), bf16[8,8,768]{2,1,0:T(8,128)(2,1)S(1)}, u32[]{:S(2)}, u32[]{:S(2)}) async-start(bf16[8,8,768]{2,1,0:T(8,128)(2,1)} %broadcast_in_dim.11), calls=%async_computation.5 | async-start | bytes 196608 | tf_op jit(solution)/shard_map/all_to_all | solution.py:11
  134.3 16.1 %copy-start = (f32[768,256]{1,0:T(8,128)S(1)}, f32[768,256]{1,0:T(8,128)}, u32[]{:S(2)}) copy-start(f32[768,256]{1,0:T(8,128)} %fusion.27) | copy-start | bytes 2359300

commit v3 on v2

--- a/solution.py
+++ b/solution.py
@@ -39,7 +39,8 @@
     sent = jnp.broadcast_to(total.astype(BF16)[None], (split,) + total.shape)
     sent, rest = lax.optimization_barrier((sent, rest))
     totals = exchange(sent, "head", groups)
-    done = meanwhile(*rest)
+    totals, pieces = lax.optimization_barrier((totals, pieces))
+    done = rest if meanwhile is None else meanwhile(*rest)
     inside = jnp.einsum("ab,brl->arl", order, pieces, preferred_element_type=F32)
     outside = jnp.sum(totals.astype(F32) * wanted[:, None, None], 0)
     back, done = lax.optimization_barrier(((inside + outside[None]).astype(BF16), done))
@@ -72,13 +73,9 @@
     rows = q.shape[0]
     causal = jnp.arange(rows)[:, None] >= jnp.arange(rows)[None, :]
     state = jnp.einsum("se,sf->ef", k, v, preferred_element_type=F32)
-
-    def inner(q, k, v, d):
-        scores = jnp.einsum("te,se->ts", q, k, preferred_element_type=F32)
-        masked = jnp.where(causal, scores, 0.0).astype(BF16)
-        return q, k, v, d, masked
-
-    carried, (q, k, v, d, masked) = carry_states(state, (q, k, v, d), inner, False, before, groups)
+    scores = jnp.einsum("te,se->ts", q, k, preferred_element_type=F32)
+    masked = jnp.where(causal, scores, 0.0).astype(BF16)
+    carried, (q, k, v, d, masked) = carry_states(state, (q, k, v, d, masked), None, False, before, groups)
     mixed = jnp.dot(q, carried, preferred_element_type=F32) + jnp.dot(masked, v, preferred_element_type=F32)
     inv = lax.rsqrt(jnp.mean(mixed * mixed, -1, keepdims=True) + 1e-05)
     normed = mixed * inv
@@ -102,8 +99,14 @@
     grad_k = jnp.einsum("sf,ef->se", v, later, preferred_element_type=F32) + within_k
     grad_v = jnp.dot(k, later, preferred_element_type=F32) + within_v
     grads = jnp.concatenate([g.astype(BF16).reshape(n_head, piece, dh) for g in (grad_q, grad_k, grad_v)], axis=1)
-    back = exchange(grads, "head").reshape(xs, heads, cores, 3 * piece, dh).transpose(0, 2, 1, 3, 4)
-    return tuple(back[:, :, :, n * piece : (n + 1) * piece].reshape(shape) for n in range(3))
+    grads = lax.optimization_barrier(grads)
+    half = dh // 2
+    back = exchange(jnp.concatenate([grads[:, :, :half], grads[:, :, half:]], axis=1), "head")
+    back = lax.optimization_barrier(jnp.concatenate([back[:, : 3 * piece], back[:, 3 * piece :]], axis=-1))
+    back = back.reshape(xs, heads, cores, 3 * piece, dh).transpose(0, 2, 3, 1, 4)
+    back = lax.optimization_barrier(back.reshape(split, 3 * piece, heads, dh))
+    back = back.transpose(0, 2, 1, 3)
+    return tuple(back[:, :, n * piece : (n + 1) * piece].reshape(shape) for n in range(3))
 
 
 def solution(mesh):

time: 197 us -> 192 us (0.975)
  blocking collectives: 161 us -> 168 us
  starting transfers between devices: 12.1 us -> 6.55 us
  waiting for transfers between devices: 6.23 us -> 1.74 us
    all_to_all x6 -> x7, blocking collectives: 161 us -> 168 us  [exchange(): return lax.all_to_all(x, axes, 0, 0, axis_index_groups=groups, tiled=True)]
    all_to_all x2 -> x1, starting transfers between devices: 12.1 us -> 6.55 us  [exchange(): return lax.all_to_all(x, axes, 0, 0, axis_index_groups=groups, tiled=True)]
    all_to_all x2 -> x1, waiting for transfers between devices: 6.23 us -> 1.74 us  [exchange(): return lax.all_to_all(x, axes, 0, 0, axis_index_groups=groups, tiled=True)]
    slice x4 -> x2, local copies, waits for them, and re-layouts: 3.15 us -> 0.51 us  [the longest x1 0.28 us: local(): back[:, :3 * piece]]
  transfers between devices with their start and end apart: 2 -> 1, of which waited for: 2 -> 1; matrix products, arithmetic and copies ran while one was open for 2% -> 2% of each run, Pallas kernels for 0% -> 0%
where the time goes in v3:
time: 192 us
  blocking collectives  168 us (88%)
  starting transfers between devices  6.55 us (3%)
  matrix products  6.25 us (3%)
  local copies, waits for them, and re-layouts  5.15 us (3%)
  other arithmetic  3.49 us (2%)
    all_to_all x7, blocking collectives, exchange(): return lax.all_to_all(x, axes, 0, 0, axis_index_groups=groups, tiled=True)  168 us
    all_to_all x1, starting transfers between devices, exchange(): return lax.all_to_all(x, axes, 0, 0, axis_index_groups=groups, tiled=True)  6.55 us
  transfers between devices with their start and end apart: 1, of which 1 were waited for; matrix products, arithmetic and copies ran while one was open for 2% of the time, Pallas kernels for 0%

profile of v3, /device:TPU:1, one launch (start us, length us, event | category | flops | bytes accessed | tf_op | source)
XLA Modules:
  0.0 191.9 jit_solution(4004794703047892931)
XLA Ops:
  0.7 1.4 fusion.13
  2.5 0.6 copy-done.3
  3.2 0.6 pad_maximum_fusion
  3.9 53.6 %all_to_all.40 = bf16[64,48,256]{2,1,0:T(8,128)(2,1)S(1)} all-to-all(bf16[64,48,256]{2,1,0:T(8,128)(2,1)S(1)} %pad_maximum_fusion), channel_id=1, replica_groups=mesh['ctx'=12,'head'=64] {'head'}, dimensions={0} | all-to-all | bytes 3145728 | tf_op jit(solution)/shard_map/all_to_all | solution.py:11
  57.5 0.5 fusion.23
  58.1 0.4 fusion.5
  58.9 0.5 select_convert_fusion.1
  59.4 23.6 %all_to_all.41 = bf16[12,8,768]{2,1,0:T(8,128)(2,1)S(1)} all-to-all(bf16[12,8,768]{2,1,0:T(8,128)(2,1)S(1)} %bitcast.106), channel_id=1, replica_groups=mesh['ctx'=12,'head'=64] {'ctx'}, dimensions={0} | all-to-all | bytes 294912 | tf_op jit(solution)/shard_map/all_to_all | solution.py:11
  83.0 9.9 %all_to_all.42 = bf16[8,8,768]{2,1,0:T(8,128)(2,1)S(1)} all-to-all(bf16[8,8,768]{2,1,0:T(8,128)(2,1)S(1)} %broadcast_in_dim.10), channel_id=1, replica_groups={{0,1,16,17,32,33,48,49},{2,3,18,19,34,35,50,51},{4,5,20,21,36,37,52,53}..., dimensions={0} | all-to-all | bytes 196608 | tf_op jit(solution)/shard_map/all_to_all | solution.py:11
  93.2 13.4 %all_to_all.43 = bf16[12,8,768]{2,1,0:T(8,128)(2,1)S(1)} all-to-all(bf16[12,8,768]{2,1,0:T(8,128)(2,1)S(1)} %copy.53), channel_id=1, replica_groups=mesh['ctx'=12,'head'=64] {'ctx'}, dimensions={0} | all-to-all | bytes 294912 | tf_op jit(solution)/shard_map/all_to_all | solution.py:11
  106.8 0.3 fusion.22
  107.1 0.5 multiply_reduce_fusion
  107.9 0.3 convolution_convert_fusion
  108.3 14.4 %all_to_all.44 = bf16[12,8,768]{2,1,0:T(8,128)(2,1)S(1)} all-to-all(bf16[12,8,768]{2,1,0:T(8,128)(2,1)S(1)} %bitcast.107), channel_id=1, replica_groups=mesh['ctx'=12,'head'=64] {'ctx'}, dimensions={0} | all-to-all | bytes 294912 | tf_op jit(solution)/shard_map/all_to_all | solution.py:11
  122.7 0.7 broadcast_in_dim.11
  123.3 6.5 %all-to-all-start.5 = ((bf16[8,8,768]{2,1,0:T(8,128)(2,1)}), bf16[8,8,768]{2,1,0:T(8,128)(2,1)S(1)}, u32[]{:S(2)}, u32[]{:S(2)}) async-start(bf16[8,8,768]{2,1,0:T(8,128)(2,1)} %broadcast_in_dim.11), calls=%async_computation.5 | async-start | bytes 196608 | tf_op jit(solution)/shard_map/all_to_all | solution.py:11
  129.9 0.3 fusion.26
  130.2 1.4 fusion.28
  131.6 0.5 select_convert_fusion
  132.1 0.5 fusion
  132.6 0.5 fusion.27
  133.1 1.7 all-to-all-done.5
  135.2 13.9 %all_to_all.45 = bf16[12,8,768]{2,1,0:T(8,128)(2,1)S(1)} all-to-all(bf16[12,8,768]{2,1,0:T(8,128)(2,1)S(1)} %copy.56), channel_id=1, replica_groups=mesh['ctx'=12,'head'=64] {'ctx'}, dimensions={0} | all-to-all | bytes 294912 | tf_op jit(solution)/shard_map/all_to_all | solution.py:11
  149.2 0.3 fusion.2
  149.6 0.3 fusion.1
  150.0 0.4 pad_maximum_fusion.1
  150.4 0.2 fusion.24
  150.7 0.3 pad_maximum_fusion.3
  151.0 39.0 %all_to_all.46 = bf16[64,72,128]{2,1,0:T(8,128)(2,1)S(1)} all-to-all(bf16[64,72,128]{2,1,0:T(8,128)(2,1)S(1)} %pad_maximum_fusion.3), channel_id=1, replica_groups=mesh['ctx'=12,'head'=64] {'head'}, dimensions={0} | all-to-all | bytes 2359296 | tf_op jit(solution)/shard_map/all_to_all | solution.py:11
  190.0 0.3 fusion.25
  190.5 0.4 copy.57
  190.9 1.0 slice_bitcast_fusion
  (37 shorter events, 2.4 us)
Async XLA Ops:
  0.6 1.6 copy-start.1
  0.6 1.7 copy-start.2
  2.1 1.0 copy-start.3
  123.3 11.6 %all-to-all-start.5 = ((bf16[8,8,768]{2,1,0:T(8,128)(2,1)}), bf16[8,8,768]{2,1,0:T(8,128)(2,1)S(1)}, u32[]{:S(2)}, u32[]{:S(2)}) async-start(bf16[8,8,768]{2,1,0:T(8,128)(2,1)} %broadcast_in_dim.11), calls=%async_computation.5 | async-start | bytes 196608 | tf_op jit(solution)/shard_map/all_to_all | solution.py:11
  133.1 16.1 %copy-start = (f32[768,256]{1,0:T(8,128)S(1)}, f32[768,256]{1,0:T(8,128)}, u32[]{:S(2)}) copy-start(f32[768,256]{1,0:T(8,128)} %fusion.28) | copy-start | bytes 2359300

commit v4 on v3

--- a/solution.py
+++ b/solution.py
@@ -35,7 +35,7 @@
     order = (at[:, None] < at[None, :] if reverse else at[:, None] > at[None, :]).astype(BF16)
     pieces, rest = lax.optimization_barrier((to_pieces(state, n_ctx), rest))
     pieces = exchange(pieces, "ctx")
-    total = jnp.sum(pieces.astype(F32), 0)
+    total = lax.optimization_barrier(jnp.sum(pieces.astype(F32), 0))
     sent = jnp.broadcast_to(total.astype(BF16)[None], (split,) + total.shape)
     sent, rest = lax.optimization_barrier((sent, rest))
     totals = exchange(sent, "head", groups)
@@ -59,14 +59,14 @@
     other = jnp.arange(split)
     before, after = ((other < row).astype(F32), (other > row).astype(F32))
 
-    def for_devices(array):
-        return array.reshape(xs, cores, heads, piece, dh).transpose(0, 2, 1, 3, 4).reshape(n_head, piece, dh)
+    def by_token(array):
+        return array.reshape(split, heads, piece, dh).transpose(0, 2, 1, 3)
 
-    gate = gates.astype(F32)
-    dnorm = out_grad.astype(F32) * gains[None, :, None, None, None, :] * jax.nn.silu(gate)
-    sent = jnp.concatenate(
-        [for_devices(queries), for_devices(keys), for_devices(values), for_devices(dnorm.astype(BF16))], axis=1
-    )
+    gate = by_token(gates).astype(F32)
+    dnorm = by_token(out_grad).astype(F32) * gains[None, None] * jax.nn.silu(gate)
+    sent = jnp.concatenate([by_token(queries), by_token(keys), by_token(values), dnorm.astype(BF16)], axis=1)
+    sent = lax.optimization_barrier(sent).reshape(xs, cores, 4 * piece, heads, dh)
+    sent = sent.transpose(0, 3, 1, 2, 4).reshape(n_head, 4 * piece, dh)
     sent, before, after = lax.optimization_barrier((sent, before, after))
     got = exchange(sent, "head")
     q, k, v, d = (got[:, n * piece : (n + 1) * piece].reshape(n_head * piece, dh) for n in range(4))

time: 192 us -> 191 us (level)
  no operation moved by 1% of the time
where the time goes in v4:
time: 191 us
  blocking collectives  168 us (88%)
  starting transfers between devices  6.55 us (3%)
  matrix products  6.25 us (3%)
  local copies, waits for them, and re-layouts  4.46 us (2%)
  other arithmetic  3.07 us (2%)
    all_to_all x7, blocking collectives, exchange(): return lax.all_to_all(x, axes, 0, 0, axis_index_groups=groups, tiled=True)  168 us
    all_to_all x1, starting transfers between devices, exchange(): return lax.all_to_all(x, axes, 0, 0, axis_index_groups=groups, tiled=True)  6.55 us
  transfers between devices with their start and end apart: 1, of which 1 were waited for; matrix products, arithmetic and copies ran while one was open for 2% of the time, Pallas kernels for 0%

profile of v4, /device:TPU:1, one launch (start us, length us, event | category | flops | bytes accessed | tf_op | source)
XLA Modules:
  0.0 190.8 jit_solution(9804931113394699844)
XLA Ops:
  0.7 1.5 fusion.11
  2.2 0.2 pad_maximum_fusion
  2.4 0.4 copy.39
  2.8 53.6 %all_to_all.40 = bf16[64,48,256]{2,1,0:T(8,128)(2,1)S(1)} all-to-all(bf16[64,48,256]{2,1,0:T(8,128)(2,1)S(1)} %bitcast.122), channel_id=1, replica_groups=mesh['ctx'=12,'head'=64] {'head'}, dimensions={0} | all-to-all | bytes 3145728 | tf_op jit(solution)/shard_map/all_to_all | solution.py:11
  56.4 0.5 fusion.26
  57.0 0.4 fusion.5
  57.8 0.5 select_convert_fusion.1
  58.3 23.6 %all_to_all.41 = bf16[12,8,768]{2,1,0:T(8,128)(2,1)S(1)} all-to-all(bf16[12,8,768]{2,1,0:T(8,128)(2,1)S(1)} %bitcast.130), channel_id=1, replica_groups=mesh['ctx'=12,'head'=64] {'ctx'}, dimensions={0} | all-to-all | bytes 294912 | tf_op jit(solution)/shard_map/all_to_all | solution.py:11
  81.9 9.8 %all_to_all.42 = bf16[8,8,768]{2,1,0:T(8,128)(2,1)S(1)} all-to-all(bf16[8,8,768]{2,1,0:T(8,128)(2,1)S(1)} %broadcast_in_dim.10), channel_id=1, replica_groups={{0,1,16,17,32,33,48,49},{2,3,18,19,34,35,50,51},{4,5,20,21,36,37,52,53}..., dimensions={0} | all-to-all | bytes 196608 | tf_op jit(solution)/shard_map/all_to_all | solution.py:11
  92.1 13.4 %all_to_all.43 = bf16[12,8,768]{2,1,0:T(8,128)(2,1)S(1)} all-to-all(bf16[12,8,768]{2,1,0:T(8,128)(2,1)S(1)} %copy.45), channel_id=1, replica_groups=mesh['ctx'=12,'head'=64] {'ctx'}, dimensions={0} | all-to-all | bytes 294912 | tf_op jit(solution)/shard_map/all_to_all | solution.py:11
  105.7 0.3 fusion.25
  106.0 0.5 multiply_reduce_fusion
  106.8 0.3 convolution_convert_fusion
  107.2 14.4 %all_to_all.44 = bf16[12,8,768]{2,1,0:T(8,128)(2,1)S(1)} all-to-all(bf16[12,8,768]{2,1,0:T(8,128)(2,1)S(1)} %bitcast.131), channel_id=1, replica_groups=mesh['ctx'=12,'head'=64] {'ctx'}, dimensions={0} | all-to-all | bytes 294912 | tf_op jit(solution)/shard_map/all_to_all | solution.py:11
  121.6 0.7 broadcast_in_dim.11
  122.2 6.5 %all-to-all-start.5 = ((bf16[8,8,768]{2,1,0:T(8,128)(2,1)}), bf16[8,8,768]{2,1,0:T(8,128)(2,1)S(1)}, u32[]{:S(2)}, u32[]{:S(2)}) async-start(bf16[8,8,768]{2,1,0:T(8,128)(2,1)} %broadcast_in_dim.11), calls=%async_computation.5 | async-start | bytes 196608 | tf_op jit(solution)/shard_map/all_to_all | solution.py:11
  128.8 0.3 fusion.29
  129.1 1.4 fusion.31
  130.5 0.5 select_convert_fusion
  131.0 0.5 fusion
  131.5 0.5 fusion.30
  132.0 1.7 all-to-all-done.5
  134.1 13.9 %all_to_all.45 = bf16[12,8,768]{2,1,0:T(8,128)(2,1)S(1)} all-to-all(bf16[12,8,768]{2,1,0:T(8,128)(2,1)S(1)} %copy.48), channel_id=1, replica_groups=mesh['ctx'=12,'head'=64] {'ctx'}, dimensions={0} | all-to-all | bytes 294912 | tf_op jit(solution)/shard_map/all_to_all | solution.py:11
  148.1 0.3 fusion.2
  148.5 0.3 fusion.1
  148.9 0.4 pad_maximum_fusion.1
  149.3 0.2 fusion.27
  149.5 0.3 pad_maximum_fusion.3
  149.9 39.0 %all_to_all.46 = bf16[64,72,128]{2,1,0:T(8,128)(2,1)S(1)} all-to-all(bf16[64,72,128]{2,1,0:T(8,128)(2,1)S(1)} %pad_maximum_fusion.3), channel_id=1, replica_groups=mesh['ctx'=12,'head'=64] {'head'}, dimensions={0} | all-to-all | bytes 2359296 | tf_op jit(solution)/shard_map/all_to_all | solution.py:11
  188.9 0.3 fusion.28
  189.3 0.4 copy.49
  189.8 1.0 slice_bitcast_fusion
  (34 shorter events, 2.0 us)
Async XLA Ops:
  0.6 1.5 copy-start.1
  0.6 1.5 copy-start.2
  0.7 1.5 copy-start.3
  122.2 11.6 %all-to-all-start.5 = ((bf16[8,8,768]{2,1,0:T(8,128)(2,1)}), bf16[8,8,768]{2,1,0:T(8,128)(2,1)S(1)}, u32[]{:S(2)}, u32[]{:S(2)}) async-start(bf16[8,8,768]{2,1,0:T(8,128)(2,1)} %broadcast_in_dim.11), calls=%async_computation.5 | async-start | bytes 196608 | tf_op jit(solution)/shard_map/all_to_all | solution.py:11
  132.0 16.1 %copy-start = (f32[768,256]{1,0:T(8,128)S(1)}, f32[768,256]{1,0:T(8,128)}, u32[]{:S(2)}) copy-start(f32[768,256]{1,0:T(8,128)} %fusion.31) | copy-start | bytes 2359300

commit v5 on v4

--- a/solution.py
+++ b/solution.py
@@ -91,7 +91,7 @@
             across, k, preferred_element_type=F32
         )
         within_k = jnp.einsum("ts,te->se", across, q, preferred_element_type=F32)
-        return k, v, grad_q.astype(BF16), within_k, within_v
+        return k, v, grad_q.astype(BF16), within_k.astype(BF16), within_v.astype(BF16)
 
     later, (k, v, grad_q, within_k, within_v) = carry_states(
         back_state, (q, k, v, masked, dmixed, carried), inner_back, True, after, groups

time: 191 us -> 191 us (level)
  no operation moved by 1% of the time
where the time goes in v5:
time: 191 us
  blocking collectives  168 us (88%)
  starting transfers between devices  6.55 us (3%)
  matrix products  6.13 us (3%)
  local copies, waits for them, and re-layouts  4.47 us (2%)
  other arithmetic  3.07 us (2%)
    all_to_all x7, blocking collectives, exchange(): return lax.all_to_all(x, axes, 0, 0, axis_index_groups=groups, tiled=True)  168 us
    all_to_all x1, starting transfers between devices, exchange(): return lax.all_to_all(x, axes, 0, 0, axis_index_groups=groups, tiled=True)  6.55 us
  transfers between devices with their start and end apart: 1, of which 1 were waited for; matrix products, arithmetic and copies ran while one was open for 2% of the time, Pallas kernels for 0%

profile of v5, /device:TPU:1, one launch (start us, length us, event | category | flops | bytes accessed | tf_op | source)
XLA Modules:
  0.0 190.7 jit_solution(7479241690321338661)
XLA Ops:
  0.7 1.5 fusion.11
  2.2 0.2 pad_maximum_fusion
  2.4 0.4 copy.39
  2.8 53.6 %all_to_all.40 = bf16[64,48,256]{2,1,0:T(8,128)(2,1)S(1)} all-to-all(bf16[64,48,256]{2,1,0:T(8,128)(2,1)S(1)} %bitcast.122), channel_id=1, replica_groups=mesh['ctx'=12,'head'=64] {'head'}, dimensions={0} | all-to-all | bytes 3145728 | tf_op jit(solution)/shard_map/all_to_all | solution.py:11
  56.4 0.5 fusion.26
  57.0 0.4 fusion.5
  57.8 0.5 select_convert_fusion.1
  58.3 23.6 %all_to_all.41 = bf16[12,8,768]{2,1,0:T(8,128)(2,1)S(1)} all-to-all(bf16[12,8,768]{2,1,0:T(8,128)(2,1)S(1)} %bitcast.130), channel_id=1, replica_groups=mesh['ctx'=12,'head'=64] {'ctx'}, dimensions={0} | all-to-all | bytes 294912 | tf_op jit(solution)/shard_map/all_to_all | solution.py:11
  81.9 9.8 %all_to_all.42 = bf16[8,8,768]{2,1,0:T(8,128)(2,1)S(1)} all-to-all(bf16[8,8,768]{2,1,0:T(8,128)(2,1)S(1)} %broadcast_in_dim.10), channel_id=1, replica_groups={{0,1,16,17,32,33,48,49},{2,3,18,19,34,35,50,51},{4,5,20,21,36,37,52,53}..., dimensions={0} | all-to-all | bytes 196608 | tf_op jit(solution)/shard_map/all_to_all | solution.py:11
  92.1 13.4 %all_to_all.43 = bf16[12,8,768]{2,1,0:T(8,128)(2,1)S(1)} all-to-all(bf16[12,8,768]{2,1,0:T(8,128)(2,1)S(1)} %copy.45), channel_id=1, replica_groups=mesh['ctx'=12,'head'=64] {'ctx'}, dimensions={0} | all-to-all | bytes 294912 | tf_op jit(solution)/shard_map/all_to_all | solution.py:11
  105.7 0.3 fusion.25
  106.0 0.5 multiply_reduce_fusion
  106.8 0.3 convolution_convert_fusion.2
  107.2 14.4 %all_to_all.44 = bf16[12,8,768]{2,1,0:T(8,128)(2,1)S(1)} all-to-all(bf16[12,8,768]{2,1,0:T(8,128)(2,1)S(1)} %bitcast.131), channel_id=1, replica_groups=mesh['ctx'=12,'head'=64] {'ctx'}, dimensions={0} | all-to-all | bytes 294912 | tf_op jit(solution)/shard_map/all_to_all | solution.py:11
  121.6 0.7 broadcast_in_dim.11
  122.2 6.5 %all-to-all-start.5 = ((bf16[8,8,768]{2,1,0:T(8,128)(2,1)}), bf16[8,8,768]{2,1,0:T(8,128)(2,1)S(1)}, u32[]{:S(2)}, u32[]{:S(2)}) async-start(bf16[8,8,768]{2,1,0:T(8,128)(2,1)} %broadcast_in_dim.11), calls=%async_computation.5 | async-start | bytes 196608 | tf_op jit(solution)/shard_map/all_to_all | solution.py:11
  128.8 1.3 convolution_convert_fusion
  130.0 0.3 fusion.29
  130.3 0.5 select_convert_fusion
  130.9 0.5 fusion
  131.4 0.5 convolution_convert_fusion.1
  131.9 1.9 all-to-all-done.5
  134.1 13.9 %all_to_all.45 = bf16[12,8,768]{2,1,0:T(8,128)(2,1)S(1)} all-to-all(bf16[12,8,768]{2,1,0:T(8,128)(2,1)S(1)} %copy.48), channel_id=1, replica_groups=mesh['ctx'=12,'head'=64] {'ctx'}, dimensions={0} | all-to-all | bytes 294912 | tf_op jit(solution)/shard_map/all_to_all | solution.py:11
  148.1 0.3 fusion.2
  148.5 0.3 fusion.1
  148.9 0.4 pad_maximum_fusion.1
  149.3 0.2 fusion.27
  149.5 0.3 pad_maximum_fusion.3
  149.9 38.9 %all_to_all.46 = bf16[64,72,128]{2,1,0:T(8,128)(2,1)S(1)} all-to-all(bf16[64,72,128]{2,1,0:T(8,128)(2,1)S(1)} %pad_maximum_fusion.3), channel_id=1, replica_groups=mesh['ctx'=12,'head'=64] {'head'}, dimensions={0} | all-to-all | bytes 2359296 | tf_op jit(solution)/shard_map/all_to_all | solution.py:11
  188.8 0.3 fusion.28
  189.2 0.4 copy.49
  189.7 1.0 slice_bitcast_fusion
  (34 shorter events, 2.0 us)
Async XLA Ops:
  0.6 1.5 copy-start
  0.6 1.5 copy-start.1
  0.7 1.5 copy-start.2
  122.2 11.6 %all-to-all-start.5 = ((bf16[8,8,768]{2,1,0:T(8,128)(2,1)}), bf16[8,8,768]{2,1,0:T(8,128)(2,1)S(1)}, u32[]{:S(2)}, u32[]{:S(2)}) async-start(bf16[8,8,768]{2,1,0:T(8,128)(2,1)} %broadcast_in_dim.11), calls=%async_computation.5 | async-start | bytes 196608 | tf_op jit(solution)/shard_map/all_to_all | solution.py:11
  131.9 16.2 %copy-start.3 = (bf16[768,256]{1,0:T(8,128)(2,1)S(1)}, bf16[768,256]{1,0:T(8,128)(2,1)}, u32[]{:S(2)}) copy-start(bf16[768,256]{1,0:T(8,128)(2,1)} %convolution_convert_fusion) | copy-start | bytes 1179652
